TPU v7x, 128 devices: a whole 4x4x4 slice. The times are simulated.
128 devices in a mesh: row: 8 (over z, core), col: 16 (over y, x).
Axes of the slice: x: 4, y: 4, z: 4, core: 2. Of those that a mesh axis runs over, the one named last changes fastest.
Arguments:
- counts: int32 [16384, 32768], P('row', 'col'), may hold values from 0 to 512
- block_mask: int32 [64, 128], P('row', 'col'), may hold values from 0 to 1
- row_perm: int32 [16384], P('row'), may hold values from 0 to 16383, as said below
- col_perm: int32 [32768], P('col'), may hold values from 0 to 32767, as said below
- row_logm: float32 [16384], P('row'), may hold values from 0 to 3
- col_logm: float32 [32768], P('col'), may hold values from 0 to 3
- row_emb: bfloat16 [16384, 512], P(('row', 'col')), may hold values from -1.1953125 to 1.1953125
- col_emb: bfloat16 [32768, 512], P(('col', 'row')), may hold values from -1.1953125 to 1.1953125
Outputs:
- row_grad: float32 [16384, 512], P(('row', 'col'))
- col_grad: float32 [32768, 512], P(('col', 'row'))
Inputs may be any that keep to these rules, and one draw needn't show every extreme that they name: `row_perm`: each aligned block of 2048 entries is a permutation of that block's own index range. `col_perm`: each aligned block of 2048 entries is a permutation of that block's own index range.
All inputs are finite; a program needn't handle non-finite values.
Results may differ from a plain program's by a relative error of at most 0.0022.
Values may be sent and summed in bfloat16 or wider, within the bound.
A program may use at most 128 MiB of HBM per device.

v0:
```python
import jax
import jax.numpy as jnp
from jax import lax
from jax.sharding import PartitionSpec as P


def cell_delta(score, count, active, row_part, col_part):
    real_count = count.astype(jnp.float32)
    safe = jnp.maximum(real_count, 1.0)
    pmi = jnp.log(safe) - row_part[:, None] - col_part[None, :]
    confid = 0.1 + 0.25 * jnp.sqrt(safe)
    positive = confid * (score - pmi)
    zeroed = jax.nn.sigmoid(score - pmi)
    deriv = jnp.where(count > 0, positive, zeroed)
    return (active.astype(jnp.float32) * deriv).astype(jnp.bfloat16)


def shards(counts, block_mask, row_perm, col_perm, row_logm, col_logm, row_emb, col_emb):
    shard_rows = counts.shape[0]
    shard_cols = counts.shape[1]
    all_cols = shard_cols * lax.axis_size("col")
    all_rows = shard_rows * lax.axis_size("row")
    block_side = shard_rows // block_mask.shape[0]
    row_group = lax.all_gather(row_emb, "col", axis=0, tiled=True)
    col_group = lax.all_gather(col_emb, "row", axis=0, tiled=True)
    row_local = row_perm - lax.axis_index("row") * shard_rows
    col_local = col_perm - lax.axis_index("col") * shard_cols
    wvec = jnp.take(row_group, row_local, axis=0)
    cvec = jnp.take(col_group, col_local, axis=0)
    score = lax.dot_general(
        wvec, cvec, (((1,), (1,)), ((), ())), preferred_element_type=jnp.float32
    )
    active = jnp.repeat(jnp.repeat(block_mask, block_side, axis=0), block_side, axis=1)
    delta = cell_delta(score, counts, active, row_logm, col_logm)
    row_scale = 1.0 / jnp.sqrt(jnp.float32(all_cols))
    col_scale = 1.0 / jnp.sqrt(jnp.float32(all_rows))
    gshard = jnp.dot(delta, cvec, preferred_element_type=jnp.float32) * row_scale
    ordered = jnp.zeros(gshard.shape, jnp.float32).at[row_local].set(gshard)
    row_grad = lax.psum_scatter(ordered, "col", scatter_dimension=0, tiled=True)
    hshard = (
        lax.dot_general(delta, wvec, (((0,), (0,)), ((), ())), preferred_element_type=jnp.float32)
        * col_scale
    )
    col_ordered = jnp.zeros(hshard.shape, jnp.float32).at[col_local].set(hshard)
    col_grad = lax.psum_scatter(col_ordered, "row", scatter_dimension=0, tiled=True)
    return (row_grad, col_grad)


def solution(mesh):
    in_specs = (
        P("row", "col"),
        P("row", "col"),
        P("row"),
        P("col"),
        P("row"),
        P("col"),
        P(("row", "col"), None),
        P(("col", "row"), None),
    )
    out_specs = (P(("row", "col"), None), P(("col", "row"), None))
    return jax.shard_map(shards, mesh=mesh, in_specs=in_specs, out_specs=out_specs, check_vma=False)
```

profile of v0, /device:TPU:1, one launch (start us, length us, event | category | flops | bytes accessed | tf_op | source)
XLA Modules:
  0.0 263.0 jit_solution(2042594573164533374)
XLA Ops:
  7.2 0.0 all-gather.5.cloned.1.call-start
  7.2 0.7 all-gather.5.cloned.1.call-update
  7.9 0.0 all-gather.3.cloned.1.call-start
  7.9 0.7 all-gather.3.cloned.1.call-update
  8.6 0.0 reduce-scatter.3.cloned.1.call-start
  8.7 0.7 convert_element_type.17
  9.4 0.1 broadcast_in_dim.24
  9.5 2.5 broadcast_in_dim.25
  11.9 0.0 copy-start.1
  11.9 0.0 copy-start.2
  11.9 11.2 %copy.10 = f32[256,8,8,256]{3,1,2,0:T(8,128)} copy(f32[256,8,8,256]{3,2,1,0:T(8,128)S(1)} %bitcast.5) | data formatting | bytes 33554432
  23.2 0.0 copy-done.1
  23.2 0.0 copy-done.2
  23.2 15.5 %all-gather.5.cloned.1.call-done = bf16[2048,512]{1,0:T(8,128)(2,1)} async-done(((bf16[256,512]{1,0:T(8,128)(2,1)}), bf16[2048,512]{1,0:T(8,128)(2,1)}) %all-gather.5.cloned.1.call-update) | async-done | bytes 2097168 | tf_op jit(solution)/shard_map/all_gather | solution.py:25
  38.8 11.1 %gather_fusion.1 = bf16[2048,512]{1,0:T(8,128)(2,1)} fusion(bf16[2048,512]{1,0:T(8,128)(2,1)} %all-gather.5.cloned.1.call-done, s32[2048]{0:T(1024)S(1)} %broadcast_clamp_fusion), kind=kCustom, calls=%fused_computation.1.clone | custom fusion | bytes 4202496 | tf_op jit(solution)/shard_map/jit(_take)/gather | solution.py:29
  49.9 0.0 copy-start.3
  49.9 0.0 copy-start.4
  49.9 35.0 %all-gather.3.cloned.1.call-done = bf16[2048,512]{1,0:T(8,128)(2,1)} async-done(((bf16[128,512]{1,0:T(8,128)(2,1)}), bf16[2048,512]{1,0:T(8,128)(2,1)}) %all-gather.3.cloned.1.call-update) | async-done | bytes 2097168 | tf_op jit(solution)/shard_map/all_gather | solution.py:24
  84.8 9.4 %gather_fusion = bf16[2048,512]{1,0:T(8,128)(2,1)S(1)} fusion(bf16[2048,512]{1,0:T(8,128)(2,1)} %all-gather.3.cloned.1.call-done, s32[2048]{0:T(1024)S(1)} %broadcast_clamp_fusion.1), kind=kCustom, calls=%fused_computation.clone | custom fusion | bytes 4202496 | tf_op jit(solution)/shard_map/jit(_take)/gather | solution.py:28
  94.3 0.0 copy-done.3
  94.3 0.0 copy-done.4
  94.3 0.0 copy-start
  94.3 24.6 %multiply_convert_fusion = bf16[2048,2048]{1,0:T(8,128)(2,1)} fusion(f32[2048,2048]{1,0:T(8,128)} %bitcast.6, s32[2048,2048]{1,0:T(8,128)} %param.10, f32[2048]{0:T(1024)S(1)} %copy-done.3, f32[2048]{0:T(1024)S(1)} %copy-done.4, bf16[2048,512]{1,0:T(8,128)(2,1)S(1)} %gather_fusion, pred[2048]{0:T(1024)(128)(4,1)S(1)} %get-tuple-element.7, ...), kind=kOutput, calls=%fused_computation.4 | convolution fusion | flops 4359979008 | bytes 46157824 | tf_op jit(solution)/shard_map/dot_general | solution.py:30
  118.9 0.0 copy-done
  118.9 10.0 %fusion.9 = f32[2048,512]{1,0:T(8,128)} fusion(bf16[2048,2048]{1,0:T(8,128)(2,1)} %multiply_convert_fusion, bf16[2048,512]{1,0:T(8,128)(2,1)S(1)} %copy-done, pred[2048]{0:T(1024)(128)(4,1)S(1)} %get-tuple-element.3), kind=kOutput, calls=%fused_computation.16 | convolution fusion | flops 4296015872 | bytes 14682112 | tf_op jit(solution)/shard_map/dot_general | solution.py:37
  128.9 12.1 %scatter_custom_fusion = f32[2048,512]{1,0:T(8,128)} fusion(s32[2048]{0:T(1024)S(1)} %get-tuple-element.8, f32[2048,512]{1,0:T(8,128)} %fusion.9, f32[]{:T(128)} %constant.16.clone.1, f32[]{:T(128)} %constant.3.clone.1), kind=kCustom, calls=%fused_computation.7 | custom fusion | flops 1048576 | bytes 8388616 | tf_op jit(solution)/shard_map/scatter | solution.py:38
  141.0 0.0 reduce-scatter.3.cloned.1.call-update
  141.0 0.0 reduce-scatter.5.cloned.1.call-start
  141.1 10.0 %fusion.8 = f32[2048,512]{1,0:T(8,128)} fusion(bf16[2048,2048]{1,0:T(8,128)(2,1)} %multiply_convert_fusion, bf16[2048,512]{1,0:T(8,128)(2,1)S(1)} %gather_fusion, pred[2048]{0:T(1024)(128)(4,1)S(1)} %get-tuple-element.7), kind=kOutput, calls=%fused_computation.15 | convolution fusion | flops 4296015872 | bytes 14682112 | tf_op jit(solution)/shard_map/dot_general | solution.py:41
  151.1 12.3 %scatter_custom_fusion.1 = f32[2048,512]{1,0:T(8,128)} fusion(s32[2048]{0:T(1024)S(1)} %get-tuple-element.4, f32[2048,512]{1,0:T(8,128)} %fusion.8, f32[]{:T(128)} %constant.17.clone.1, f32[]{:T(128)} %constant.3.clone.1), kind=kCustom, calls=%fused_computation.5 | custom fusion | flops 1048576 | bytes 8388616 | tf_op jit(solution)/shard_map/scatter | solution.py:44
  163.4 0.0 reduce-scatter.5.cloned.1.call-update
  163.4 53.8 %reduce-scatter.3.cloned.1.call-done = f32[128,512]{1,0:T(8,128)} async-done(((f32[2048,512]{1,0:T(8,128)}), f32[128,512]{1,0:T(8,128)}) %reduce-scatter.3.cloned.1.call-update) | async-done | bytes 262160 | tf_op jit(solution)/shard_map/reduce_scatter | solution.py:39
  217.2 39.3 %reduce-scatter.5.cloned.1.call-done = f32[256,512]{1,0:T(8,128)} async-done(((f32[2048,512]{1,0:T(8,128)}), f32[256,512]{1,0:T(8,128)}) %reduce-scatter.5.cloned.1.call-update) | async-done | bytes 524304 | tf_op jit(solution)/shard_map/reduce_scatter | solution.py:45
  (3 shorter events, 0.0 us)
Async XLA Ops:
  7.2 31.6 %all-gather.5.cloned.1.call-start = ((), (), s32[]{:S(2)}) async-start(), calls=%async_computation.3 | async-start | bytes 2359296 | tf_op jit(solution)/shard_map/all_gather | solution.py:25
  7.9 77.0 %all-gather.3.cloned.1.call-start = ((), (), s32[]{:S(2)}) async-start(), calls=%async_computation.2 | async-start | bytes 2228224 | tf_op jit(solution)/shard_map/all_gather | solution.py:24
  8.6 208.6 %reduce-scatter.3.cloned.1.call-start = ((), (), s32[]{:S(2)}) async-start(), calls=%async_computation.4 | async-start | bytes 4456448 | tf_op jit(solution)/shard_map/reduce_scatter | solution.py:39
  11.9 11.2 %copy-start.1 = (s32[2048]{0:T(1024)S(1)}, s32[2048]{0:T(1024)}, u32[]{:S(2)}) copy-start(s32[2048]{0:T(1024)} %param.13) | copy-start | bytes 24580
  11.9 11.2 %copy-start.2 = (s32[2048]{0:T(1024)S(1)}, s32[2048]{0:T(1024)}, u32[]{:S(2)}) copy-start(s32[2048]{0:T(1024)} %param.12) | copy-start | bytes 24580
  49.9 44.4 %copy-start.3 = (f32[2048]{0:T(1024)S(1)}, f32[2048]{0:T(1024)}, u32[]{:S(2)}) copy-start(f32[2048]{0:T(1024)} %param.15) | copy-start | bytes 24580
  49.9 44.4 %copy-start.4 = (f32[2048]{0:T(1024)S(1)}, f32[2048]{0:T(1024)}, u32[]{:S(2)}) copy-start(f32[2048]{0:T(1024)} %param.14) | copy-start | bytes 24580
  94.3 24.6 %copy-start = (bf16[2048,512]{1,0:T(8,128)(2,1)S(1)}, bf16[2048,512]{1,0:T(8,128)(2,1)}, u32[]{:S(2)}) copy-start(bf16[2048,512]{1,0:T(8,128)(2,1)} %gather_fusion.1) | copy-start | bytes 6291460
  141.0 115.4 %reduce-scatter.5.cloned.1.call-start = ((), (), s32[]{:S(2)}) async-start(), calls=%async_computation.5 | async-start | bytes 4718592 | tf_op jit(solution)/shard_map/reduce_scatter | solution.py:45
Sparse Core Ops, SparseCore 0:
  9.7 28.9 all-gather.4
  40.9 43.9 all-gather.2
  141.1 76.0 reduce-scatter.2
  220.2 36.2 reduce-scatter.4
where the time goes:
time: 266 us; the launch traced here: 263 us
  waiting for transfers between devices  145 us (55%)
  matrix products  44.6 us (17%)
  local copies, waits for them, and re-layouts  34.4 us (13%)
  other arithmetic  25.1 us (9%)
  between operations  13.8 us (5%)
    reduce_scatter x1, waiting for transfers between devices, shards(): row_grad = lax.psum_scatter(ordered, 'col', scatter_dimension=0, tiled=True)  53.8 us
    reduce_scatter x1, waiting for transfers between devices, shards(): lax.psum_scatter(col_ordered, 'row', scatter_dimension=0, tiled=True)  39.3 us
    all_gather x1, waiting for transfers between devices, shards(): row_group = lax.all_gather(row_emb, 'col', axis=0, tiled=True)  35 us
    dot_general x1, matrix products, shards(): lax.dot_general(wvec, cvec, (((1,), (1,)), ((), ())), preferred_element_t...  24.6 us
    all_gather x1, waiting for transfers between devices, shards(): col_group = lax.all_gather(col_emb, 'row', axis=0, tiled=True)  15.5 us
    scatter x1, other arithmetic, shards(): col_ordered = jnp.zeros(hshard.shape, jnp.float32).at[col_local].set(hshard)  12.3 us
    scatter x1, other arithmetic, shards(): ordered = jnp.zeros(gshard.shape, jnp.float32).at[row_local].set(gshard)  12.1 us
    unnamed x11, local copies, waits for them, and re-layouts  11.2 us
  transfers between devices with their start and end apart: 4, of which 4 were waited for; matrix products, arithmetic and copies ran while one was open for 18% of the time, Pallas kernels for 0%

commit v1 on v0

v1 whole, which is shorter than its diff:
```python
import functools

import jax
import jax.numpy as jnp
from jax import lax
from jax.experimental import pallas as pl
from jax.experimental.pallas import tpu as pltpu
from jax.sharding import PartitionSpec as P

MESH = pl.DeviceIdType.MESH
F32 = jnp.float32
BF16 = jnp.bfloat16

SR = 2048
D = 512
HALF = 256
BLK = 256
T = 512
NT = (((1,), (1,)), ((), ()))
NN = (((1,), (0,)), ((), ()))


def dot(a, b, dims):
    return lax.dot_general(a, b, dims, preferred_element_type=F32)


def kernel(
    g_scale, h_scale,
    counts, mask, rperm, cperm, rlog, clog, remb, cemb,
    rout, cout,
    cbuf, rg, cg, vec, vcol, wvec, wt, cvec, delta,
    gs, gord, r1, s2, r2,
    hown, hsend, hrecv, hb, hord, rz, fsend, frecv,
    csem, xs, xr, ys, yr, zs, zr, ks, kr, lsem,
    g1s, g1r, g2s, g2r, hks, hkr, hzs, hzr, fsm, frm,
):
    row = lax.axis_index("row")
    col = lax.axis_index("col")
    z, core = row // 2, row % 2
    y, x = col // 4, col % 4
    row0, col0 = row * SR, col * SR

    def dev(zz, kk, yy, xx):
        return ((zz % 4) * 2 + kk, (yy % 4) * 4 + (xx % 4))

    def at_x(d):
        return dev(z, core, y, x + d)

    def at_y(d):
        return dev(z, core, y + d, x)

    def at_z(d):
        return dev(z + d, core, y, x)

    sibling = dev(z, 1 - core, y, x)

    def send(src, dst, ssem, rsem, to):
        c = pltpu.make_async_remote_copy(
            src_ref=src, dst_ref=dst, send_sem=ssem, recv_sem=rsem, device_id=to, device_id_type=MESH
        )
        c.start()
        return c

    def got(ref, rsem, ssem):
        pltpu.make_async_remote_copy(
            src_ref=ref, dst_ref=ref, send_sem=ssem, recv_sem=rsem, device_id=sibling, device_id_type=MESH
        ).wait_recv()

    loads = []
    for i in range(4):
        c = pltpu.make_async_copy(counts.at[pl.ds(i * T, T)], cbuf.at[pl.ds(i * T, T)], csem.at[i])
        c.start()
        loads.append(c)

    barrier = pltpu.get_barrier_semaphore()
    partners = [at_x(d) for d in (1, 2, 3)] + [at_y(d) for d in (1, 2, 3)] + [at_z(d) for d in (1, 2, 3)] + [sibling]
    for to in partners:
        pl.semaphore_signal(barrier, inc=1, device_id=to, device_id_type=MESH)
    pl.semaphore_wait(barrier, len(partners))

    sent = []

    def zblk(d):
        return cg.at[(z + d) % 4, core]

    own_c = pltpu.make_async_copy(cemb, zblk(0), lsem.at[0])
    own_c.start()
    own_rows = []
    for h in range(2):
        c = pltpu.make_async_copy(remb.at[pl.ds(64 * h, 64)], rg.at[y, x, h], lsem.at[1 + h])
        c.start()
        own_rows.append(c)
    sent.append(send(cemb, zblk(0), zs.at[0], zr.at[0], at_z(1)))
    sent.append(send(cemb, zblk(0), zs.at[1], zr.at[1], at_z(3)))
    sent.append(send(cemb, zblk(0), ks.at[0], kr.at[0], sibling))

    def blk(h, first, second):
        if h == 0:
            return rg.at[(y + second) % 4, (x + first) % 4, h]
        return rg.at[(y + first) % 4, (x + second) % 4, h]

    def first_axis(h, d):
        return at_x(d) if h == 0 else at_y(d)

    def second_axis(h, d):
        return at_y(d) if h == 0 else at_x(d)

    for h in range(2):
        own = remb.at[pl.ds(64 * h, 64)]
        sent.append(send(own, blk(h, 0, 0), xs.at[h, 0], xr.at[h, 0], first_axis(h, 1)))
        sent.append(send(own, blk(h, 0, 0), xs.at[h, 1], xr.at[h, 1], first_axis(h, 3)))
    for h in range(2):
        own = remb.at[pl.ds(64 * h, 64)]
        sent.append(send(own, blk(h, 0, 0), ys.at[h, 0, 0], yr.at[h, 0, 0], second_axis(h, 1)))
        sent.append(send(own, blk(h, 0, 0), ys.at[h, 0, 1], yr.at[h, 0, 1], second_axis(h, 3)))

    lo, hi = pl.ds(0, 32), pl.ds(32, 32)
    for h in range(2):
        got(blk(h, 3, 0), xr.at[h, 0], xs.at[h, 0])
        sent.append(send(blk(h, 3, 0).at[lo], blk(h, 3, 0).at[lo], xs.at[h, 2], xr.at[h, 2], first_axis(h, 1)))
        got(blk(h, 1, 0), xr.at[h, 1], xs.at[h, 1])
        sent.append(send(blk(h, 1, 0).at[hi], blk(h, 1, 0).at[hi], xs.at[h, 3], xr.at[h, 3], first_axis(h, 3)))
    for h in range(2):
        for k, f in ((1, 3), (2, 1)):
            sent.append(send(blk(h, f, 0), blk(h, f, 0), ys.at[h, k, 0], yr.at[h, k, 0], second_axis(h, 1)))
            sent.append(send(blk(h, f, 0), blk(h, f, 0), ys.at[h, k, 1], yr.at[h, k, 1], second_axis(h, 3)))
    zlo, zhi = pl.ds(0, 128), pl.ds(128, 128)
    got(zblk(3), zr.at[0], zs.at[0])
    sent.append(send(zblk(3).at[zlo], zblk(3).at[zlo], zs.at[2], zr.at[2], at_z(1)))
    sent.append(send(zblk(3), zblk(3), ks.at[1], kr.at[1], sibling))
    got(zblk(1), zr.at[1], zs.at[1])
    sent.append(send(zblk(1).at[zhi], zblk(1).at[zhi], zs.at[3], zr.at[3], at_z(3)))
    sent.append(send(zblk(1), zblk(1), ks.at[2], kr.at[2], sibling))
    for h in range(2):
        got(blk(h, 2, 0).at[lo], xr.at[h, 2], xs.at[h, 2])
        got(blk(h, 2, 0).at[hi], xr.at[h, 3], xs.at[h, 3])
        sent.append(send(blk(h, 2, 0), blk(h, 2, 0), ys.at[h, 3, 0], yr.at[h, 3, 0], second_axis(h, 1)))
        sent.append(send(blk(h, 2, 0), blk(h, 2, 0), ys.at[h, 3, 1], yr.at[h, 3, 1], second_axis(h, 3)))
    firsts = (0, 3, 1, 2)
    for k in range(4):
        for h in range(2):
            f = firsts[k]
            got(blk(h, f, 3), yr.at[h, k, 0], ys.at[h, k, 0])
            sent.append(send(blk(h, f, 3).at[lo], blk(h, f, 3).at[lo], ys.at[h, k, 2], yr.at[h, k, 2], second_axis(h, 1)))
            got(blk(h, f, 1), yr.at[h, k, 1], ys.at[h, k, 1])
            sent.append(send(blk(h, f, 1).at[hi], blk(h, f, 1).at[hi], ys.at[h, k, 3], yr.at[h, k, 3], second_axis(h, 3)))
    got(zblk(2).at[zlo], zr.at[2], zs.at[2])
    got(zblk(2).at[zhi], zr.at[3], zs.at[3])
    sent.append(send(zblk(2), zblk(2), ks.at[3], kr.at[3], sibling))

    vec[...] = jnp.zeros_like(vec)
    vec[0:1, :] = (rperm[...] - row0).astype(F32)
    vec[1:2, :] = (cperm[...] - col0).astype(F32)
    vec[2:3, :] = rlog[...]

    def turn(i, _):
        o = pl.multiple_of(i * 128, 128)
        vcol[pl.ds(o, 128), :] = jnp.transpose(vec[:, pl.ds(o, 128)])
        return 0

    lax.fori_loop(0, 16, turn, 0)

    own_c.wait()
    for k, d in enumerate((0, 3, 1, 2)):
        got(cg.at[(z + d) % 4, 1 - core], kr.at[k], ks.at[k])

    lane = lax.broadcasted_iota(jnp.int32, (T, SR), 1).astype(F32)

    def pick(i, which, src):
        o = pl.multiple_of(i * T, T)
        hot = jnp.where(vcol[pl.ds(o, T), which : which + 1] == lane, 1.0, 0.0).astype(BF16)
        return dot(hot, src, NN).astype(BF16)

    def pick_c(i, _):
        cvec[pl.ds(pl.multiple_of(i * T, T), T), :] = pick(i, 1, cg[...].reshape(SR, D))
        return 0

    lax.fori_loop(0, 4, pick_c, 0)

    for c in own_rows:
        c.wait()
    for k in range(4):
        for h in range(2):
            f = firsts[k]
            got(blk(h, f, 2).at[lo], yr.at[h, k, 2], ys.at[h, k, 2])
            got(blk(h, f, 2).at[hi], yr.at[h, k, 3], ys.at[h, k, 3])

    def pick_w(i, _):
        o = pl.multiple_of(i * T, T)
        w = pick(i, 0, rg[...].reshape(SR, D))
        wvec[pl.ds(o, T), :] = w
        for h in range(2):
            wt[(core + h) % 2, :, pl.ds(o, T)] = jnp.transpose(w[:, HALF * h : HALF * (h + 1)])
        return 0

    lax.fori_loop(0, 4, pick_w, 0)

    for c in loads:
        c.wait()

    def cells(t, _):
        i, j = t // 4, t % 4
        ro = pl.multiple_of(i * T, T)
        co = pl.multiple_of(j * T, T)
        score = dot(wvec[pl.ds(ro, T), :], cvec[pl.ds(co, T), :], NT)
        for a in range(2):
            for b in range(2):
                ra = pl.multiple_of(ro + a * BLK, BLK)
                cb = pl.multiple_of(co + b * BLK, BLK)
                count = cbuf[pl.ds(ra, BLK), pl.ds(cb, BLK)].astype(F32)
                safe = jnp.maximum(count, 1.0)
                base = vcol[pl.ds(ra, BLK), 2:3] + clog[:, pl.ds(cb, BLK)]
                u = score[a * BLK : (a + 1) * BLK, b * BLK : (b + 1) * BLK] - (jnp.log(safe) - base)
                pos = (0.1 + 0.25 * (safe * lax.rsqrt(safe))) * u
                zero = 0.5 * jnp.tanh(0.5 * u) + 0.5
                on = mask[i * 2 + a, j * 2 + b].astype(F32)
                delta[pl.ds(ra, BLK), pl.ds(cb, BLK)] = (on * jnp.where(count > 0.0, pos, zero)).astype(BF16)
        return 0

    lax.fori_loop(0, 16, cells, 0)

    kcopies = []
    for j in range(4):
        js = pl.ds(j * T, T)
        ht = dot(wt[...].reshape(D, SR), delta[:, js], NN) * h_scale
        hown[j] = ht[:HALF]
        hsend[j] = ht[HALF:]
        kcopies.append(send(hsend.at[j], hrecv.at[j], hks.at[j], hkr.at[j], sibling))
    sent += kcopies

    sub = lax.broadcasted_iota(jnp.int32, (T, SR), 0).astype(F32)

    def spread(k, which):
        at = vec[which : which + 1, :] - lax.convert_element_type(k * T, F32)
        return jnp.where(sub == at, 1.0, 0.0).astype(BF16)

    def row_terms(ch):
        def terms(i, _):
            o = pl.multiple_of(i * T, T)
            gs[pl.ds(o, T), :] = (
                dot(delta[pl.ds(o, T), :], cvec[:, HALF * ch : HALF * (ch + 1)], NN) * g_scale
            ).astype(BF16)
            return 0

        lax.fori_loop(0, 4, terms, 0)

        def order(k, _):
            gord[ch, k] = dot(spread(k, 0), gs[...], NN).astype(BF16).reshape(4, 2, 64, HALF)
            return 0

        lax.fori_loop(0, 4, order, 0)
        for d in (2, 1, 3):
            sent.append(send(gord.at[ch, (y + d) % 4, :, 0], r1.at[ch, 0, d - 1], g1s.at[ch, 0, d - 1], g1r.at[ch, 0, d - 1], at_y(d)))
            sent.append(send(gord.at[ch, :, (x + d) % 4, 1], r1.at[ch, 1, d - 1], g1s.at[ch, 1, d - 1], g1r.at[ch, 1, d - 1], at_x(d)))

    row_terms(0)

    for j in range(4):
        got(hrecv.at[j], hkr.at[j], hks.at[j])
        hb[:, j * T : (j + 1) * T] = (hown[j] + hrecv[j]).astype(BF16)

    def order_c(k, _):
        hord[k] = dot(spread(k, 1), hb[...], NT).astype(BF16).reshape(2, BLK, HALF)
        return 0

    lax.fori_loop(0, 4, order_c, 0)
    for d in (2, 1, 3):
        sent.append(send(hord.at[(z + d) % 4], rz.at[d - 1], hzs.at[d - 1], hzr.at[d - 1], at_z(d)))

    row_terms(1)

    def row_sums(ch):
        for h in range(2):
            for d in range(3):
                got(r1.at[ch, h, d], g1r.at[ch, h, d], g1s.at[ch, h, d])
            mine = gord[ch, y, :, 0] if h == 0 else gord[ch, :, x, 1]
            total = mine.astype(F32)
            for d in range(3):
                total = total + r1[ch, h, d].astype(F32)
            s2[ch, h] = total
            here = x if h == 0 else y
            for d in (2, 1, 3):
                sent.append(send(s2.at[ch, h, (here + d) % 4], r2.at[ch, h, d - 1], g2s.at[ch, h, d - 1], g2r.at[ch, h, d - 1], second(h, d)))

    def second(h, d):
        return at_x(d) if h == 0 else at_y(d)

    row_sums(0)
    row_sums(1)

    for d in range(3):
        got(rz.at[d], hzr.at[d], hzs.at[d])

    def col_total(k):
        total = hord[z, k].astype(F32)
        for d in range(3):
            total = total + rz[d, k].astype(F32)
        return total

    fsend[...] = col_total(1 - core)
    sent.append(send(fsend, frecv, fsm, frm, sibling))
    cout[core] = col_total(core)

    for ch in range(2):
        for h in range(2):
            for d in range(3):
                got(r2.at[ch, h, d], g2r.at[ch, h, d], g2s.at[ch, h, d])
            here = x if h == 0 else y
            total = s2[ch, h, here]
            for d in range(3):
                total = total + r2[ch, h, d]
            rout[h * 64 : (h + 1) * 64, ch * HALF : (ch + 1) * HALF] = total

    got(frecv, frm, fsm)
    cout[1 - core] = frecv[...]
    for c in sent:
        c.wait_send()


def shards(counts, block_mask, row_perm, col_perm, row_logm, col_logm, row_emb, col_emb):
    all_cols = counts.shape[1] * lax.axis_size("col")
    all_rows = counts.shape[0] * lax.axis_size("row")
    vm = pl.BlockSpec(memory_space=pltpu.VMEM)
    dma = pltpu.SemaphoreType.DMA
    V = pltpu.VMEM
    rout, cout = pl.pallas_call(
        functools.partial(kernel, float(all_cols) ** -0.5, float(all_rows) ** -0.5),
        out_shape=(
            jax.ShapeDtypeStruct((128, D), F32),
            jax.ShapeDtypeStruct((2, BLK, HALF), F32),
        ),
        in_specs=[pl.BlockSpec(memory_space=pl.ANY), pl.BlockSpec(memory_space=pltpu.SMEM)] + [vm] * 6,
        out_specs=(vm, vm),
        scratch_shapes=[
            V((SR, SR), jnp.int32),
            V((4, 4, 2, 64, D), BF16),
            V((4, 2, BLK, D), BF16),
            V((8, SR), F32),
            V((SR, 8), F32),
            V((SR, D), BF16),
            V((2, HALF, SR), BF16),
            V((SR, D), BF16),
            V((SR, SR), BF16),
            V((SR, HALF), BF16),
            V((2, 4, 4, 2, 64, HALF), BF16),
            V((2, 2, 3, 4, 64, HALF), BF16),
            V((2, 2, 4, 64, HALF), F32),
            V((2, 2, 3, 64, HALF), F32),
            V((4, HALF, T), F32),
            V((4, HALF, T), F32),
            V((4, HALF, T), F32),
            V((HALF, SR), BF16),
            V((4, 2, BLK, HALF), BF16),
            V((3, 2, BLK, HALF), BF16),
            V((BLK, HALF), F32),
            V((BLK, HALF), F32),
            dma((4,)),
            dma((2, 4)), dma((2, 4)),
            dma((2, 4, 4)), dma((2, 4, 4)),
            dma((4,)), dma((4,)),
            dma((4,)), dma((4,)),
            dma((3,)),
            dma((2, 2, 3)), dma((2, 2, 3)),
            dma((2, 2, 3)), dma((2, 2, 3)),
            dma((4,)), dma((4,)),
            dma((3,)), dma((3,)),
            dma, dma,
        ],
        compiler_params=pltpu.CompilerParams(
            collective_id=0, has_side_effects=True, vmem_limit_bytes=63 * 1024 * 1024
        ),
        cost_estimate=pl.CostEstimate(flops=26_000_000_000, bytes_accessed=20_000_000, transcendentals=12_000_000),
    )(
        counts, block_mask, row_perm.reshape(1, SR), col_perm.reshape(1, SR),
        row_logm.reshape(1, SR), col_logm.reshape(1, SR), row_emb, col_emb,
    )
    return rout, cout.transpose(1, 0, 2).reshape(BLK, D)


def solution(mesh):
    in_specs = (
        P("row", "col"),
        P("row", "col"),
        P("row"),
        P("col"),
        P("row"),
        P("col"),
        P(("row", "col"), None),
        P(("col", "row"), None),
    )
    out_specs = (P(("row", "col"), None), P(("col", "row"), None))
    return jax.shard_map(shards, mesh=mesh, in_specs=in_specs, out_specs=out_specs, check_vma=False)
```

time: 266 us -> 89.2 us (0.34); the launches traced: 263 us -> 89 us
  waiting for transfers between devices: 145 us -> 0 us
  Pallas kernels: 0 us -> 84.4 us
  matrix products: 44.6 us -> 0 us
  local copies, waits for them, and re-layouts: 34.4 us -> 3.9 us
  other arithmetic: 25.1 us -> 0 us
  between operations: 13.8 us -> 0.65 us
    reduce_scatter x2 -> x0, waiting for transfers between devices: 93 us -> none  [the longest x1 53.8 us: shards(): row_grad = lax.psum_scatter(ordered, 'col', scatter_dimension=0, tiled=True)]
    pallas_call x0 -> x1, Pallas kernels: none -> 84.4 us  [shards(): pl.pallas_call(functools.partial(kernel, float(all_cols) ** (-0.5), float...]
    all_gather x2 -> x0, waiting for transfers between devices: 50.5 us -> none  [the longest x1 35 us: shards(): row_group = lax.all_gather(row_emb, 'col', axis=0, tiled=True)]
    dot_general x3 -> x0, matrix products: 44.6 us -> none  [the longest x1 24.6 us: shards(): lax.dot_general(wvec, cvec, (((1,), (1,)), ((), ())), preferred_element_t...]
    scatter x2 -> x0, other arithmetic: 24.4 us -> none  [the longest x1 12.3 us: shards(): col_ordered = jnp.zeros(hshard.shape, jnp.float32).at[col_local].set(hshard)]
    gather x2 -> x0, local copies, waits for them, and re-layouts: 20.6 us -> none  [the longest x1 11.1 us: shards(): cvec = jnp.take(col_group, col_local, axis=0)]
    unnamed x11 -> x2, local copies, waits for them, and re-layouts: 11.2 us -> 2.67 us
  transfers between devices with their start and end apart: 4 -> 0, of which waited for: 4 -> 0; matrix products, arithmetic and copies ran while one was open for 18% -> 0% of each run, Pallas kernels for 0% -> 0%
where the time goes in v1:
time: 89.2 us; the launch traced here: 89 us
  Pallas kernels  84.4 us (95%)
  local copies, waits for them, and re-layouts  3.9 us (4%)
    pallas_call x1, Pallas kernels, shards(): pl.pallas_call(functools.partial(kernel, float(all_cols) ** (-0.5), float...  84.4 us
    unnamed x2, local copies, waits for them, and re-layouts  2.67 us

profile of v1, /device:TPU:1, one launch (start us, length us, event | category | flops | bytes accessed | tf_op | source)
XLA Modules:
  0.0 89.0 jit_solution(11573138183125032101)
XLA Ops:
  0.6 84.4 %shard_map.95 = (f32[128,512]{1,0:T(8,128)}, f32[2,256,256]{2,1,0:T(8,128)}) custom-call(s32[2048,2048]{1,0:T(8,128)} %counts.1, s32[8,8]{1,0:T(8,128)} %mask.1, s32[1,2048]{1,0:T(1,128)} %bitcast.8, s32[1,2048]{1,0:T(1,128)} %bitcast.9, f32[1,2048]{1,0:T(1,128)} %bitcast.10, f32[1,2048]{1,0:T(1,128)} %bitcast.11, bf16[128,512]{1,0:T(8,128)(2,1)} %remb.1, ...), custom_call_target="tpu_custom_call" | custom-call | flops 25999998976 | bytes 20000000 | tf_op jit(solution)/shard_map/pallas_call | solution.py:326
  85.1 1.2 %copy.10 = f32[256,2,256]{0,2,1:T(8,128)S(1)} copy(f32[256,2,256]{2,0,1:T(8,128)} %bitcast.7) | data formatting | bytes 1048576 | tf_op jit(solution)/shard_map/transpose | solution.py:377
  86.3 1.0 %copy.11 = f32[256,512]{1,0:T(8,128)} copy(f32[256,512]{0,1:T(8,128)S(1)} %bitcast.6) | data formatting | bytes 1048576
  87.3 1.7 %copy.13 = f32[128,512]{1,0:T(8,128)} copy(f32[128,512]{1,0:T(8,128)} %get-tuple-element.10) | data formatting | bytes 524288

commit v2 on v1

--- a/solution.py
+++ b/solution.py
@@ -29,7 +29,7 @@
     counts, mask, rperm, cperm, rlog, clog, remb, cemb,
     rout, cout,
     cbuf, rg, cg, vec, vcol, wvec, wt, cvec, delta,
-    gs, gord, r1, s2, r2,
+    gs, gord, r1, s2, s2b, r2,
     hown, hsend, hrecv, hb, hord, rz, fsend, frecv,
     csem, xs, xr, ys, yr, zs, zr, ks, kr, lsem,
     g1s, g1r, g2s, g2r, hks, hkr, hzs, hzr, fsm, frm,
@@ -198,26 +198,22 @@
     for c in loads:
         c.wait()
 
-    def cells(t, _):
-        i, j = t // 4, t % 4
-        ro = pl.multiple_of(i * T, T)
-        co = pl.multiple_of(j * T, T)
-        score = dot(wvec[pl.ds(ro, T), :], cvec[pl.ds(co, T), :], NT)
-        for a in range(2):
-            for b in range(2):
-                ra = pl.multiple_of(ro + a * BLK, BLK)
-                cb = pl.multiple_of(co + b * BLK, BLK)
-                count = cbuf[pl.ds(ra, BLK), pl.ds(cb, BLK)].astype(F32)
-                safe = jnp.maximum(count, 1.0)
-                base = vcol[pl.ds(ra, BLK), 2:3] + clog[:, pl.ds(cb, BLK)]
-                u = score[a * BLK : (a + 1) * BLK, b * BLK : (b + 1) * BLK] - (jnp.log(safe) - base)
-                pos = (0.1 + 0.25 * (safe * lax.rsqrt(safe))) * u
-                zero = 0.5 * jnp.tanh(0.5 * u) + 0.5
-                on = mask[i * 2 + a, j * 2 + b].astype(F32)
-                delta[pl.ds(ra, BLK), pl.ds(cb, BLK)] = (on * jnp.where(count > 0.0, pos, zero)).astype(BF16)
-        return 0
-
-    lax.fori_loop(0, 16, cells, 0)
+    def cells(j, _):
+        at = pl.ds(pl.multiple_of(j * BLK, BLK), BLK)
+        score = dot(wvec[...], cvec[at, :], NT)
+        for i in range(8):
+            rows = slice(i * BLK, (i + 1) * BLK)
+            count = cbuf[rows, at].astype(F32)
+            safe = jnp.maximum(count, 1.0)
+            base = vcol[rows, 2:3] + clog[:, at]
+            u = score[rows] - (jnp.log(safe) - base)
+            pos = (0.1 + 0.25 * (safe * lax.rsqrt(safe))) * u
+            zero = 0.5 * jnp.tanh(0.5 * u) + 0.5
+            on = mask[i, j].astype(F32)
+            delta[rows, at] = (on * jnp.where(count > 0.0, pos, zero)).astype(BF16)
+        return 0
+
+    lax.fori_loop(0, 8, cells, 0)
 
     kcopies = []
     for j in range(4):
@@ -278,9 +274,10 @@
             for d in range(3):
                 total = total + r1[ch, h, d].astype(F32)
             s2[ch, h] = total
+            s2b[ch, h] = total.astype(BF16)
             here = x if h == 0 else y
             for d in (2, 1, 3):
-                sent.append(send(s2.at[ch, h, (here + d) % 4], r2.at[ch, h, d - 1], g2s.at[ch, h, d - 1], g2r.at[ch, h, d - 1], second(h, d)))
+                sent.append(send(s2b.at[ch, h, (here + d) % 4], r2.at[ch, h, d - 1], g2s.at[ch, h, d - 1], g2r.at[ch, h, d - 1], second(h, d)))
 
     def second(h, d):
         return at_x(d) if h == 0 else at_y(d)
@@ -299,7 +296,7 @@
 
     fsend[...] = col_total(1 - core)
     sent.append(send(fsend, frecv, fsm, frm, sibling))
-    cout[core] = col_total(core)
+    cout[:, pl.ds(pl.multiple_of(core * HALF, HALF), HALF)] = col_total(core)
 
     for ch in range(2):
         for h in range(2):
@@ -308,11 +305,11 @@
             here = x if h == 0 else y
             total = s2[ch, h, here]
             for d in range(3):
-                total = total + r2[ch, h, d]
+                total = total + r2[ch, h, d].astype(F32)
             rout[h * 64 : (h + 1) * 64, ch * HALF : (ch + 1) * HALF] = total
 
     got(frecv, frm, fsm)
-    cout[1 - core] = frecv[...]
+    cout[:, pl.ds(pl.multiple_of((1 - core) * HALF, HALF), HALF)] = frecv[...]
     for c in sent:
         c.wait_send()
 
@@ -327,7 +324,7 @@
         functools.partial(kernel, float(all_cols) ** -0.5, float(all_rows) ** -0.5),
         out_shape=(
             jax.ShapeDtypeStruct((128, D), F32),
-            jax.ShapeDtypeStruct((2, BLK, HALF), F32),
+            jax.ShapeDtypeStruct((BLK, D), F32),
         ),
         in_specs=[pl.BlockSpec(memory_space=pl.ANY), pl.BlockSpec(memory_space=pltpu.SMEM)] + [vm] * 6,
         out_specs=(vm, vm),
@@ -345,7 +342,8 @@
             V((2, 4, 4, 2, 64, HALF), BF16),
             V((2, 2, 3, 4, 64, HALF), BF16),
             V((2, 2, 4, 64, HALF), F32),
-            V((2, 2, 3, 64, HALF), F32),
+            V((2, 2, 4, 64, HALF), BF16),
+            V((2, 2, 3, 64, HALF), BF16),
             V((4, HALF, T), F32),
             V((4, HALF, T), F32),
             V((4, HALF, T), F32),
@@ -374,7 +372,7 @@
         counts, block_mask, row_perm.reshape(1, SR), col_perm.reshape(1, SR),
         row_logm.reshape(1, SR), col_logm.reshape(1, SR), row_emb, col_emb,
     )
-    return rout, cout.transpose(1, 0, 2).reshape(BLK, D)
+    return rout, cout
 
 
 def solution(mesh):

time: 89.2 us -> 83.9 us (0.941)
  Pallas kernels: 84.4 us -> 79.5 us
    pallas_call x1, Pallas kernels: 84.4 us -> 79.5 us  [shards(): pl.pallas_call(functools.partial(kernel, float(all_cols) ** (-0.5), float...]
    transpose x1 -> x0, local copies, waits for them, and re-layouts: 1.24 us -> none  [shards(): return (rout, cout.transpose(1, 0, 2).reshape(BLK, D))]
where the time goes in v2:
time: 83.9 us; the launch traced here: 83.7 us
  Pallas kernels  79.5 us (95%)
  local copies, waits for them, and re-layouts  3.54 us (4%)
    pallas_call x1, Pallas kernels, shards(): pl.pallas_call(functools.partial(kernel, float(all_cols) ** (-0.5), float...  79.5 us
    unnamed x2, local copies, waits for them, and re-layouts  3.54 us

profile of v2, /device:TPU:1, one launch (start us, length us, event | category | flops | bytes accessed | tf_op | source)
XLA Modules:
  0.0 83.7 jit_solution(10857058915751462524)
XLA Ops:
  0.6 79.5 %shard_map.95 = (f32[128,512]{1,0:T(8,128)}, f32[256,512]{1,0:T(8,128)}) custom-call(s32[2048,2048]{1,0:T(8,128)} %counts.1, s32[8,8]{1,0:T(8,128)} %mask.1, s32[1,2048]{1,0:T(1,128)} %bitcast.4, s32[1,2048]{1,0:T(1,128)} %bitcast.5, f32[1,2048]{1,0:T(1,128)} %bitcast.6, f32[1,2048]{1,0:T(1,128)} %bitcast.7, bf16[128,512]{1,0:T(8,128)(2,1)} %remb.1, ...), custom_call_target="tpu_custom_call" | custom-call | flops 25999998976 | bytes 20000000 | tf_op jit(solution)/shard_map/pallas_call | solution.py:323
  80.2 1.7 %copy.12 = f32[128,512]{1,0:T(8,128)} copy(f32[128,512]{1,0:T(8,128)} %get-tuple-element.4) | data formatting | bytes 524288
  81.8 1.9 %copy.13 = f32[256,512]{1,0:T(8,128)} copy(f32[256,512]{1,0:T(8,128)} %get-tuple-element.5) | data formatting | bytes 1048576
